TPU v7x, 256 devices: a whole 4x4x8 slice. The times are simulated.
256 devices in a mesh: face: 16 (over y, x_hi, core), fsdp: 16 (over z, x_lo).
Axes of the slice: x: 4 (x_hi: 2, x_lo: 2; x = x_hi * 2 + x_lo), y: 4, z: 8, core: 2. Of those that a mesh axis runs over, the one named last changes fastest.
Arguments:
- node_features: bfloat16 [98304, 1024], P(('face', 'fsdp')), may hold values from -120 to 120
- norm_gain: float32 [1024], replicated, may hold values from 0.1 to 1.9
- query_weight: bfloat16 [1024, 1024], P('fsdp'), may hold values from -0.2 to 0.2
- key_weight: bfloat16 [1024, 1024], P('fsdp'), may hold values from -6 to 6
- value_weight: bfloat16 [1024, 1024], P('fsdp'), may hold values from -0.1875 to 0.1875
- out_weight: bfloat16 [1024, 1024], P('fsdp'), may hold values from -3 to 3
- cotangent: bfloat16 [98304, 1024], P(('face', 'fsdp')), may hold values from -24 to 24
- pair_mask: int32 [768, 6], P(('face', 'fsdp')), may hold values from 0 to 1, as said below
- border_ids: int32 [256, 3], P(('face', 'fsdp')), may hold values from 0 to 2
Outputs:
- layer_update: bfloat16 [98304, 1024], P(('face', 'fsdp'))
- node_gradient: bfloat16 [98304, 1024], P(('face', 'fsdp'))
- query_gradient: float32 [1024, 1024], P('fsdp')
- key_gradient: float32 [1024, 1024], P('fsdp')
- value_gradient: float32 [1024, 1024], P('fsdp')
- output_gradient: float32 [1024, 1024], P('fsdp')
Inputs may be any that keep to these rules, and one draw needn't show every extreme that they name: `pair_mask`: each query tile lists its own tile (the key slot equal to its index within the device), and query tile b mod 3 lists the border slot 3 + b.
All inputs are finite; a program needn't handle non-finite values.
Results may differ from a plain program's by a relative error of at most 0.03.
The roundings to bfloat16 on the way count: a program that leaves them out, or rounds other values in their place, can miss the bound.
Values may be sent and summed in bfloat16 or wider, within the bound.
No kernel may reach another device: no remote copies, remote signals or barrier semaphores. Data moves between devices by JAX's collectives and lax.ppermute only.
A program may use at most 128 MiB of HBM per device.

v0:
```python
import jax
import jax.numpy as jnp
from jax import lax
from jax.sharding import PartitionSpec as P

HEADS = 16
MATCHINGS = 3


epsilon = 1e-06
group_heads = 4


def partner(block, axis, distance):
    count = lax.axis_size(axis)
    route = []
    for low in range(count):
        high = low | 1 << distance
        if high != low and high < count:
            route += [(low, high), (high, low)]
    return lax.ppermute(block, axis, route)


def attend(queries, key_set, value_set, grad_rows, live, head_count):
    row_count, feature_count = queries.shape
    key_count = key_set.shape[0]
    head_width = feature_count // head_count
    block_width = group_heads * head_width
    factor = head_width ** (-0.5)
    mask_all = live[None]

    def head_step(step_index, carry):
        out_acc, query_acc, key_acc, value_acc = carry
        offset = step_index * block_width
        query_part = lax.dynamic_slice_in_dim(queries, offset, block_width, 1).reshape(
            row_count, group_heads, head_width
        )
        key_part = lax.dynamic_slice_in_dim(key_set, offset, block_width, 1).reshape(
            key_count, group_heads, head_width
        )
        value_part = lax.dynamic_slice_in_dim(value_set, offset, block_width, 1).reshape(
            key_count, group_heads, head_width
        )
        grad_part = lax.dynamic_slice_in_dim(grad_rows, offset, block_width, 1).reshape(
            row_count, group_heads, head_width
        )
        scores = (
            jnp.einsum("ihd,jhd->hij", query_part, key_part, preferred_element_type=jnp.float32)
            * factor
        )
        top_score = jnp.max(jnp.where(mask_all, scores, -jnp.inf), axis=2, keepdims=True)
        expo_terms = jnp.exp(jnp.where(mask_all, scores - top_score, -jnp.inf))
        weights = expo_terms / jnp.sum(expo_terms, axis=2, keepdims=True)
        probs = weights.astype(jnp.bfloat16)
        attended = jnp.einsum("hij,jhd->ihd", probs, value_part, preferred_element_type=jnp.float32)
        grad_probs = jnp.einsum(
            "ihd,jhd->hij", grad_part, value_part, preferred_element_type=jnp.float32
        )
        inner_sum = jnp.sum(weights * grad_probs, axis=2, keepdims=True)
        grad_scores = (weights * (grad_probs - inner_sum) * factor).astype(jnp.bfloat16)
        grad_query = jnp.einsum(
            "hij,jhd->ihd", grad_scores, key_part, preferred_element_type=jnp.float32
        )
        grad_key = jnp.einsum(
            "hij,ihd->jhd", grad_scores, query_part, preferred_element_type=jnp.float32
        )
        grad_value = jnp.einsum(
            "hij,ihd->jhd", probs, grad_part, preferred_element_type=jnp.float32
        )
        out_acc = lax.dynamic_update_slice_in_dim(
            out_acc, attended.reshape(row_count, block_width), offset, 1
        )
        query_acc = lax.dynamic_update_slice_in_dim(
            query_acc, grad_query.reshape(row_count, block_width), offset, 1
        )
        key_acc = lax.dynamic_update_slice_in_dim(
            key_acc, grad_key.reshape(key_count, block_width), offset, 1
        )
        value_acc = lax.dynamic_update_slice_in_dim(
            value_acc, grad_value.reshape(key_count, block_width), offset, 1
        )
        return (out_acc, query_acc, key_acc, value_acc)

    start_state = (
        jnp.zeros((row_count, feature_count), jnp.float32),
        jnp.zeros((row_count, feature_count), jnp.float32),
        jnp.zeros((key_count, feature_count), jnp.float32),
        jnp.zeros((key_count, feature_count), jnp.float32),
    )
    return lax.fori_loop(0, head_count // group_heads, head_step, start_state)


def contract_rows(left, right):
    return lax.dot_general(
        left, right, (((0,), (0,)), ((), ())), preferred_element_type=jnp.float32
    )


def times_transpose(left, right):
    return lax.dot_general(
        left, right, (((1,), (1,)), ((), ())), preferred_element_type=jnp.float32
    )


def local(
    node_features,
    norm_gain,
    query_weight,
    key_weight,
    value_weight,
    out_weight,
    cotangent,
    pair_mask,
    border_ids,
):
    row_count, feature_count = node_features.shape
    tile_count = pair_mask.shape[0]
    tile_rows = row_count // tile_count
    full_query, full_key, full_value = (
        lax.all_gather(query_weight, "fsdp", axis=0, tiled=True),
        lax.all_gather(key_weight, "fsdp", axis=0, tiled=True),
        lax.all_gather(value_weight, "fsdp", axis=0, tiled=True),
    )
    full_out = lax.all_gather(out_weight, "fsdp", axis=0, tiled=True)
    features = node_features.astype(jnp.float32)
    inverse = lax.rsqrt(jnp.mean(features * features, axis=1, keepdims=True) + epsilon)
    normed = (features * inverse * norm_gain).astype(jnp.bfloat16)
    queries = jnp.dot(normed, full_query, preferred_element_type=jnp.float32).astype(jnp.bfloat16)
    keys = jnp.dot(normed, full_key, preferred_element_type=jnp.float32).astype(jnp.bfloat16)
    values = jnp.dot(normed, full_value, preferred_element_type=jnp.float32).astype(jnp.bfloat16)
    border_rows = border_ids[0]
    key_parts = [keys]
    value_parts = [values]
    for bit_number in range(MATCHINGS):
        offset = border_rows[bit_number] * tile_rows
        sent_keys = lax.dynamic_slice_in_dim(keys, offset, tile_rows, 0)
        sent_values = lax.dynamic_slice_in_dim(values, offset, tile_rows, 0)
        arrived_keys, arrived_values = partner((sent_keys, sent_values), "face", bit_number)
        key_parts.append(arrived_keys)
        value_parts.append(arrived_values)
    key_set = jnp.concatenate(key_parts, axis=0)
    value_set = jnp.concatenate(value_parts, axis=0)
    live = jnp.repeat(jnp.repeat(pair_mask, tile_rows, axis=0), tile_rows, axis=1) > 0
    grad_attended = times_transpose(cotangent, full_out).astype(jnp.bfloat16)
    attended, query_acc, key_acc, value_acc = attend(
        queries, key_set, value_set, grad_attended, live, HEADS
    )
    attended = attended.astype(jnp.bfloat16)
    layer_update = jnp.dot(attended, full_out, preferred_element_type=jnp.float32).astype(
        jnp.bfloat16
    )
    grad_queries = query_acc.astype(jnp.bfloat16)
    returned_keys = []
    returned_values = []
    for bit_number in range(MATCHINGS):
        lower = row_count + bit_number * tile_rows
        back_keys = key_acc[lower : lower + tile_rows].astype(jnp.bfloat16)
        back_values = value_acc[lower : lower + tile_rows].astype(jnp.bfloat16)
        got_keys, got_values = partner((back_keys, back_values), "face", bit_number)
        returned_keys.append(got_keys)
        returned_values.append(got_values)
    selector = (border_rows[:, None] == jnp.arange(tile_count, dtype=jnp.int32)[None, :]).astype(
        jnp.bfloat16
    )
    extra_keys = jnp.einsum(
        "bt,bnd->tnd", selector, jnp.stack(returned_keys), preferred_element_type=jnp.float32
    ).reshape(row_count, feature_count)
    extra_values = jnp.einsum(
        "bt,bnd->tnd", selector, jnp.stack(returned_values), preferred_element_type=jnp.float32
    ).reshape(row_count, feature_count)
    grad_keys = (key_acc[:row_count] + extra_keys).astype(jnp.bfloat16)
    grad_values = (value_acc[:row_count] + extra_values).astype(jnp.bfloat16)
    grad_normed = (
        times_transpose(grad_queries, full_query)
        + times_transpose(grad_keys, full_key)
        + times_transpose(grad_values, full_value)
    )
    scaled = grad_normed * norm_gain
    inner_mean = jnp.mean(scaled * features, axis=1, keepdims=True)
    node_gradient = (inverse * scaled - features * inverse**3 * inner_mean).astype(jnp.bfloat16)
    terms = (
        contract_rows(normed, grad_queries),
        contract_rows(normed, grad_keys),
        contract_rows(normed, grad_values),
        contract_rows(attended, cotangent),
    )
    shards = (
        lax.psum_scatter(
            terms[0].astype(jnp.bfloat16), "fsdp", scatter_dimension=0, tiled=True
        ).astype(jnp.float32),
        lax.psum_scatter(
            terms[1].astype(jnp.bfloat16), "fsdp", scatter_dimension=0, tiled=True
        ).astype(jnp.float32),
        lax.psum_scatter(
            terms[2].astype(jnp.bfloat16), "fsdp", scatter_dimension=0, tiled=True
        ).astype(jnp.float32),
        lax.psum_scatter(
            terms[3].astype(jnp.bfloat16), "fsdp", scatter_dimension=0, tiled=True
        ).astype(jnp.float32),
    )
    gradients = (
        lax.psum(shards[0].astype(jnp.bfloat16), "face").astype(jnp.float32),
        lax.psum(shards[1].astype(jnp.bfloat16), "face").astype(jnp.float32),
        lax.psum(shards[2].astype(jnp.bfloat16), "face").astype(jnp.float32),
        lax.psum(shards[3].astype(jnp.bfloat16), "face").astype(jnp.float32),
    )
    return (layer_update, node_gradient, gradients[0], gradients[1], gradients[2], gradients[3])


def solution(mesh):
    return jax.shard_map(
        local,
        mesh=mesh,
        in_specs=(
            P(("face", "fsdp"), None),
            P(),
            P("fsdp", None),
            P("fsdp", None),
            P("fsdp", None),
            P("fsdp", None),
            P(("face", "fsdp"), None),
            P(("face", "fsdp"), None),
            P(("face", "fsdp"), None),
        ),
        out_specs=(
            P(("face", "fsdp"), None),
            P(("face", "fsdp"), None),
            P("fsdp", None),
            P("fsdp", None),
            P("fsdp", None),
            P("fsdp", None),
        ),
        check_vma=False,
    )
```

profile of v0, /device:TPU:1, one launch (start us, length us, event | category | flops | bytes accessed | tf_op | source)
XLA Modules:
  0.0 986.8 jit_solution(13941735136232635705)
XLA Ops:
  16.2 61.3 %all-gather.5.cloned.1.call-done = bf16[1024,1024]{1,0:T(8,128)(2,1)} async-done(((bf16[64,1024]{1,0:T(8,128)(2,1)}), bf16[1024,1024]{1,0:T(8,128)(2,1)}) %all-gather.5.cloned.1.call-update) | async-done | bytes 2097168 | tf_op jit(solution)/shard_map/all_gather | solution.py:122
  77.5 2.9 convolution_convert_fusion.8
  81.3 11.0 %collective-permute-start = (bf16[128,1024]{1,0:T(8,128)(2,1)}, bf16[128,1024]{1,0:T(8,128)(2,1)S(1)}, u32[]{:S(2)}, u32[]{:S(2)}) collective-permute-start(bf16[128,1024]{1,0:T(8,128)(2,1)} %get-tuple-element.284), channel_id=1, source_target_pairs={{0,16},{16,0},{32,48},{48,32},{64,80},{80,64},{96,112},{112,96},{1... | collective-permute-start | bytes 786440 | tf_op jit(solution)/shard_map/ppermute | solution.py:21
  95.2 55.3 %all-gather.9.cloned.1.call-done = bf16[1024,1024]{1,0:T(8,128)(2,1)} async-done(((bf16[64,1024]{1,0:T(8,128)(2,1)}), bf16[1024,1024]{1,0:T(8,128)(2,1)}) %all-gather.9.cloned.1.call-update) | async-done | bytes 2097168 | tf_op jit(solution)/shard_map/all_gather | solution.py:121
  150.5 2.6 convolution_convert_fusion.6
  154.1 9.2 collective-permute-start.3
  165.3 57.9 %all-gather.7.cloned.1.call-done = bf16[1024,1024]{1,0:T(8,128)(2,1)} async-done(((bf16[64,1024]{1,0:T(8,128)(2,1)}), bf16[1024,1024]{1,0:T(8,128)(2,1)}) %all-gather.7.cloned.1.call-update) | async-done | bytes 2097168 | tf_op jit(solution)/shard_map/all_gather | solution.py:120
  223.1 3.5 convolution_convert_fusion.7
  226.6 2.7 collective-permute-start.4
  229.4 66.8 %all-gather.11.cloned.1.call-done = bf16[1024,1024]{1,0:T(8,128)(2,1)} async-done(((bf16[64,1024]{1,0:T(8,128)(2,1)}), bf16[1024,1024]{1,0:T(8,128)(2,1)}) %all-gather.11.cloned.1.call-update) | async-done | bytes 2097168 | tf_op jit(solution)/shard_map/all_gather | solution.py:124
  296.2 3.5 convolution_convert_fusion.5
  310.4 198.8 %while.20 = (s32[]{:T(128)}, bf16[384,1024]{0,1:T(8,128)(2,1)}, bf16[384,1024]{0,1:T(8,128)(2,1)}, f32[768,1024]{1,0:T(8,128)}, f32[768,1024]{1,0:T(8,128)}, /*i...) while((s32[]{:T(128)}, bf16[384,1024]{0,1:T(8,128)(2,1)}, ...), condition=%wide.region_5.6_spmd.clone, body=%wide.region_1.5_spmd.clone.sunk | while | flops 1085281536 | bytes 74744328 | solution.py:90
  316.1 4.4 fusion.143
  320.5 4.1 fusion.145
  325.7 3.0 fusion.142
  328.7 15.0 %fusion.144 = bf16[4,64,384]{2,1,0:T(8,128)(2,1)S(1)} fusion(bf16[768,4,64]{0,2,1:T(8,128)(2,1)S(1)} %bitcast.122, f32[4,384,768]{2,1,0:T(8,128)} %fusion.142, f32[4,384,768]{2,1,0:T(8,128)} %get-tuple-element.361, f32[4,384]{1,0:T(4,128)S(1)} %get-tuple-element.362), kind=kOutput, calls=%fused_computation.11.clone.1 | convolution fusion | flops 159254784 | bytes 10033152 | tf_op jit(solution)/shard_map/while/body/eval_jaxpr/hij,jhd->ihd/dot_general | solution.py:61
  343.7 14.4 %fusion.147 = f32[4,64,768]{2,1,0:T(8,128)S(1)} fusion(bf16[384,4,64]{0,2,1:T(8,128)(2,1)S(1)} %bitcast.124, f32[4,384,768]{2,1,0:T(8,128)} %fusion.142, f32[4,384,768]{2,1,0:T(8,128)} %get-tuple-element.361, f32[4,384]{1,0:T(4,128)S(1)} %get-tuple-element.362), kind=kOutput, calls=%fused_computation.10.clone.1 | convolution fusion | flops 159254784 | bytes 10426368 | tf_op jit(solution)/shard_map/while/body/eval_jaxpr/hij,ihd->jhd/dot_general | solution.py:64
  365.7 4.4 fusion.143
  370.1 4.1 fusion.145
  375.3 3.0 fusion.142
  378.2 15.0 %fusion.144 = bf16[4,64,384]{2,1,0:T(8,128)(2,1)S(1)} fusion(bf16[768,4,64]{0,2,1:T(8,128)(2,1)S(1)} %bitcast.122, f32[4,384,768]{2,1,0:T(8,128)} %fusion.142, f32[4,384,768]{2,1,0:T(8,128)} %get-tuple-element.361, f32[4,384]{1,0:T(4,128)S(1)} %get-tuple-element.362), kind=kOutput, calls=%fused_computation.11.clone.1 | convolution fusion | flops 159254784 | bytes 10033152 | tf_op jit(solution)/shard_map/while/body/eval_jaxpr/hij,jhd->ihd/dot_general | solution.py:61
  393.3 14.4 %fusion.147 = f32[4,64,768]{2,1,0:T(8,128)S(1)} fusion(bf16[384,4,64]{0,2,1:T(8,128)(2,1)S(1)} %bitcast.124, f32[4,384,768]{2,1,0:T(8,128)} %fusion.142, f32[4,384,768]{2,1,0:T(8,128)} %get-tuple-element.361, f32[4,384]{1,0:T(4,128)S(1)} %get-tuple-element.362), kind=kOutput, calls=%fused_computation.10.clone.1 | convolution fusion | flops 159254784 | bytes 10426368 | tf_op jit(solution)/shard_map/while/body/eval_jaxpr/hij,ihd->jhd/dot_general | solution.py:64
  415.3 4.4 fusion.143
  419.7 4.1 fusion.145
  424.9 3.0 fusion.142
  427.8 15.0 %fusion.144 = bf16[4,64,384]{2,1,0:T(8,128)(2,1)S(1)} fusion(bf16[768,4,64]{0,2,1:T(8,128)(2,1)S(1)} %bitcast.122, f32[4,384,768]{2,1,0:T(8,128)} %fusion.142, f32[4,384,768]{2,1,0:T(8,128)} %get-tuple-element.361, f32[4,384]{1,0:T(4,128)S(1)} %get-tuple-element.362), kind=kOutput, calls=%fused_computation.11.clone.1 | convolution fusion | flops 159254784 | bytes 10033152 | tf_op jit(solution)/shard_map/while/body/eval_jaxpr/hij,jhd->ihd/dot_general | solution.py:61
  442.9 14.4 %fusion.147 = f32[4,64,768]{2,1,0:T(8,128)S(1)} fusion(bf16[384,4,64]{0,2,1:T(8,128)(2,1)S(1)} %bitcast.124, f32[4,384,768]{2,1,0:T(8,128)} %fusion.142, f32[4,384,768]{2,1,0:T(8,128)} %get-tuple-element.361, f32[4,384]{1,0:T(4,128)S(1)} %get-tuple-element.362), kind=kOutput, calls=%fused_computation.10.clone.1 | convolution fusion | flops 159254784 | bytes 10426368 | tf_op jit(solution)/shard_map/while/body/eval_jaxpr/hij,ihd->jhd/dot_general | solution.py:64
  464.9 4.4 fusion.143
  469.2 4.1 fusion.145
  474.5 3.0 fusion.142
  477.4 15.0 %fusion.144 = bf16[4,64,384]{2,1,0:T(8,128)(2,1)S(1)} fusion(bf16[768,4,64]{0,2,1:T(8,128)(2,1)S(1)} %bitcast.122, f32[4,384,768]{2,1,0:T(8,128)} %fusion.142, f32[4,384,768]{2,1,0:T(8,128)} %get-tuple-element.361, f32[4,384]{1,0:T(4,128)S(1)} %get-tuple-element.362), kind=kOutput, calls=%fused_computation.11.clone.1 | convolution fusion | flops 159254784 | bytes 10033152 | tf_op jit(solution)/shard_map/while/body/eval_jaxpr/hij,jhd->ihd/dot_general | solution.py:61
  492.5 14.4 %fusion.147 = f32[4,64,768]{2,1,0:T(8,128)S(1)} fusion(bf16[384,4,64]{0,2,1:T(8,128)(2,1)S(1)} %bitcast.124, f32[4,384,768]{2,1,0:T(8,128)} %fusion.142, f32[4,384,768]{2,1,0:T(8,128)} %get-tuple-element.361, f32[4,384]{1,0:T(4,128)S(1)} %get-tuple-element.362), kind=kOutput, calls=%fused_computation.10.clone.1 | convolution fusion | flops 159254784 | bytes 10426368 | tf_op jit(solution)/shard_map/while/body/eval_jaxpr/hij,ihd->jhd/dot_general | solution.py:64
  509.2 3.9 convolution_convert_fusion
  513.2 2.8 convolution_convert_fusion.3
  518.4 11.1 %collective-permute-start.9 = (bf16[128,1024]{1,0:T(8,128)(2,1)S(1)}, bf16[128,1024]{1,0:T(8,128)(2,1)S(1)}, u32[]{:S(2)}, u32[]{:S(2)}) collective-permute-start(bf16[128,1024]{1,0:T(8,128)(2,1)S(1)} %get-tuple-element.275), channel_id=1, source_target_pairs={{0,16},{16,0},{32,48},{48,32},{64,80},{80,64},{96,112},{112,96},{1... | collective-permute-start | bytes 786440 | tf_op jit(solution)/shard_map/ppermute | solution.py:21
  532.8 4.7 collective-permute-done.11
  537.9 7.3 collective-permute-done.10
  550.7 2.7 convolution_convert_fusion.1
  555.7 3.4 collective-permute-start.6
  559.9 2.8 collective-permute-start.7
  563.1 3.9 collective-permute-done.8
  567.4 11.6 %collective-permute-done.7 = bf16[128,1024]{1,0:T(8,128)(2,1)S(1)} collective-permute-done((bf16[128,1024]{1,0:T(8,128)(2,1)S(1)}, bf16[128,1024]{1,0:T(8,128)(2,1)S(1)}, u32[]{:S(2)}, u32[]{:S(2)}) %collective-permute-start.7) | collective-permute-done | bytes 262176 | tf_op jit(solution)/shard_map/ppermute | solution.py:21
  584.5 2.8 convolution_convert_fusion.2
  588.3 3.6 convolution_convert_fusion.4
  597.0 66.5 %reduce-scatter.5.cloned.1.call-done = bf16[64,1024]{1,0:T(8,128)(2,1)} async-done(((bf16[1024,1024]{1,0:T(8,128)(2,1)}), bf16[64,1024]{1,0:T(8,128)(2,1)}) %reduce-scatter.5.cloned.1.call-update) | async-done | bytes 131088 | tf_op jit(solution)/shard_map/reduce_scatter | solution.py:188
  663.5 76.8 %reduce-scatter.9.cloned.1.call-done = bf16[64,1024]{1,0:T(8,128)(2,1)} async-done(((bf16[1024,1024]{1,0:T(8,128)(2,1)}), bf16[64,1024]{1,0:T(8,128)(2,1)}) %reduce-scatter.9.cloned.1.call-update) | async-done | bytes 131088 | tf_op jit(solution)/shard_map/reduce_scatter | solution.py:194
  740.3 76.6 %reduce-scatter.7.cloned.1.call-done = bf16[64,1024]{1,0:T(8,128)(2,1)} async-done(((bf16[1024,1024]{1,0:T(8,128)(2,1)}), bf16[64,1024]{1,0:T(8,128)(2,1)}) %reduce-scatter.7.cloned.1.call-update) | async-done | bytes 131088 | tf_op jit(solution)/shard_map/reduce_scatter | solution.py:191
  818.2 155.3 %all-reduce.3.cloned.1.call-done = (bf16[64,1024]{1,0:T(8,128)(2,1)}, bf16[64,1024]{1,0:T(8,128)(2,1)}, bf16[64,1024]{1,0:T(8,128)(2,1)}, bf16[64,1024]{1,0:T(8,128)(2,1)}) async-done(((bf16[64,1024]{1,0:T(8,128)(2,1)}, bf16[64,1024]{1,0:T(8,128)(2,1)}, bf16[64,1024]{1,0:T(8,128)(2,1)}, bf16[64,1024]{1,0:T(8,128)(2,1)}), (bf16[64,1024]{1,0:T(8,128)(2,1)}, bf16[64,1024]{1,0:T(8,128)(2,1)}, ...) | async-done | bytes 524304 | tf_op jit(solution)/shard_map/psum | solution.py:202
  (189 shorter events, 93.7 us)
Async XLA Ops:
  7.2 289.0 %copy-start = (bf16[384,1024]{1,0:T(8,128)(2,1)S(1)}, bf16[384,1024]{1,0:T(8,128)(2,1)}, u32[]{:S(2)}) copy-start(bf16[384,1024]{1,0:T(8,128)(2,1)} %param.17) | copy-start | bytes 2359300
  7.2 70.3 %all-gather.5.cloned.1.call-start = ((), (), s32[]{:S(2)}) async-start(), calls=%async_computation.4 | async-start | bytes 2228224 | tf_op jit(solution)/shard_map/all_gather | solution.py:122
  7.9 142.6 %all-gather.9.cloned.1.call-start = ((), (), s32[]{:S(2)}) async-start(), calls=%async_computation.6 | async-start | bytes 2228224 | tf_op jit(solution)/shard_map/all_gather | solution.py:121
  8.7 214.5 %all-gather.7.cloned.1.call-start = ((), (), s32[]{:S(2)}) async-start(), calls=%async_computation.5 | async-start | bytes 2228224 | tf_op jit(solution)/shard_map/all_gather | solution.py:120
  9.4 286.8 %all-gather.11.cloned.1.call-start = ((), (), s32[]{:S(2)}) async-start(), calls=%async_computation.7 | async-start | bytes 2228224 | tf_op jit(solution)/shard_map/all_gather | solution.py:124
  10.0 587.0 %reduce-scatter.11.cloned.1.call-start = ((), (), s32[]{:S(2)}) async-start(), calls=%async_computation.11 | async-start | bytes 2228224 | tf_op jit(solution)/shard_map/reduce_scatter | solution.py:197
  16.2 206.9 %copy-start.14 = (f32[384]{0:T(512)}, f32[384]{0:T(512)S(1)}, u32[]{:S(2)}) copy-start(f32[384]{0:T(512)S(1)} %get-tuple-element.288) | copy-start | bytes 4612
  77.5 73.1 %copy-start.3 = (bf16[384,1024]{1,0:T(8,128)(2,1)S(1)}, bf16[384,1024]{1,0:T(8,128)(2,1)}, u32[]{:S(2)}) copy-start(bf16[384,1024]{1,0:T(8,128)(2,1)} %param.11) | copy-start | bytes 2359300
  77.5 73.1 %copy-start.17 = (f32[1024]{0:T(1024)S(1)}, f32[1024]{0:T(1024)}, u32[]{:S(2)}) copy-start(f32[1024]{0:T(1024)} %param.12) | copy-start | bytes 12292
  81.3 145.3 %collective-permute-start = (bf16[128,1024]{1,0:T(8,128)(2,1)}, bf16[128,1024]{1,0:T(8,128)(2,1)S(1)}, u32[]{:S(2)}, u32[]{:S(2)}) collective-permute-start(bf16[128,1024]{1,0:T(8,128)(2,1)} %get-tuple-element.284), channel_id=1, source_target_pairs={{0,16},{16,0},{32,48},{48,32},{64,80},{80,64},{96,112},{112,96},{1... | collective-permute-start | bytes 786440 | tf_op jit(solution)/shard_map/ppermute | solution.py:21
  92.3 207.4 %collective-permute-start.2 = (bf16[128,1024]{1,0:T(8,128)(2,1)}, bf16[128,1024]{1,0:T(8,128)(2,1)}, u32[]{:S(2)}, u32[]{:S(2)}) collective-permute-start(bf16[128,1024]{1,0:T(8,128)(2,1)} %get-tuple-element.285), channel_id=1, source_target_pairs={{0,64},{64,0},{16,80},{80,16},{32,96},{96,32},{48,112},{112,48},{1... | collective-permute-start | bytes 786440 | tf_op jit(solution)/shard_map/ppermute | solution.py:21
  92.7 207.0 %collective-permute-start.1 = (bf16[128,1024]{1,0:T(8,128)(2,1)}, bf16[128,1024]{1,0:T(8,128)(2,1)}, u32[]{:S(2)}, u32[]{:S(2)}) collective-permute-start(bf16[128,1024]{1,0:T(8,128)(2,1)} %get-tuple-element.286), channel_id=1, source_target_pairs={{0,32},{32,0},{16,48},{48,16},{64,96},{96,64},{80,112},{112,80},{1... | collective-permute-start | bytes 786440 | tf_op jit(solution)/shard_map/ppermute | solution.py:21
  154.1 148.1 %collective-permute-start.3 = (bf16[128,1024]{1,0:T(8,128)(2,1)}, bf16[128,1024]{1,0:T(8,128)(2,1)}, u32[]{:S(2)}, u32[]{:S(2)}) collective-permute-start(bf16[128,1024]{1,0:T(8,128)(2,1)} %get-tuple-element.281), channel_id=1, source_target_pairs={{0,16},{16,0},{32,48},{48,32},{64,80},{80,64},{96,112},{112,96},{1... | collective-permute-start | bytes 786440 | tf_op jit(solution)/shard_map/ppermute | solution.py:21
  163.3 138.9 %collective-permute-start.5 = (bf16[128,1024]{1,0:T(8,128)(2,1)}, bf16[128,1024]{1,0:T(8,128)(2,1)}, u32[]{:S(2)}, u32[]{:S(2)}) collective-permute-start(bf16[128,1024]{1,0:T(8,128)(2,1)} %get-tuple-element.282), channel_id=1, source_target_pairs={{0,64},{64,0},{16,80},{80,16},{32,96},{96,32},{48,112},{112,48},{1... | collective-permute-start | bytes 786440 | tf_op jit(solution)/shard_map/ppermute | solution.py:21
  226.6 75.5 %collective-permute-start.4 = (bf16[128,1024]{1,0:T(8,128)(2,1)}, bf16[128,1024]{1,0:T(8,128)(2,1)S(1)}, u32[]{:S(2)}, u32[]{:S(2)}) collective-permute-start(bf16[128,1024]{1,0:T(8,128)(2,1)} %get-tuple-element.283), channel_id=1, source_target_pairs={{0,32},{32,0},{16,48},{48,16},{64,96},{96,64},{80,112},{112,80},{1... | collective-permute-start | bytes 786440 | tf_op jit(solution)/shard_map/ppermute | solution.py:21
  320.5 4.1 copy-start.21
  343.7 14.7 %copy-start.5 = (bf16[4,64,384]{2,1,0:T(8,128)(2,1)S(1)}, bf16[4,64,384]{2,1,0:T(8,128)(2,1)}, u32[]{:S(2)}) copy-start(bf16[4,64,384]{2,1,0:T(8,128)(2,1)} %fusion.145) | copy-start | bytes 589828 | tf_op jit(solution)/shard_map/while
  370.1 4.1 copy-start.21
  393.3 14.7 %copy-start.5 = (bf16[4,64,384]{2,1,0:T(8,128)(2,1)S(1)}, bf16[4,64,384]{2,1,0:T(8,128)(2,1)}, u32[]{:S(2)}) copy-start(bf16[4,64,384]{2,1,0:T(8,128)(2,1)} %fusion.145) | copy-start | bytes 589828 | tf_op jit(solution)/shard_map/while
  419.7 4.1 copy-start.21
  442.9 14.7 %copy-start.5 = (bf16[4,64,384]{2,1,0:T(8,128)(2,1)S(1)}, bf16[4,64,384]{2,1,0:T(8,128)(2,1)}, u32[]{:S(2)}) copy-start(bf16[4,64,384]{2,1,0:T(8,128)(2,1)} %fusion.145) | copy-start | bytes 589828 | tf_op jit(solution)/shard_map/while
  469.2 4.1 copy-start.21
  492.5 14.7 %copy-start.5 = (bf16[4,64,384]{2,1,0:T(8,128)(2,1)S(1)}, bf16[4,64,384]{2,1,0:T(8,128)(2,1)}, u32[]{:S(2)}) copy-start(bf16[4,64,384]{2,1,0:T(8,128)(2,1)} %fusion.145) | copy-start | bytes 589828 | tf_op jit(solution)/shard_map/while
  509.2 3.9 copy-start.4
  509.2 4.0 copy-start.10
  509.2 4.0 copy-start.15
  509.2 4.0 copy-start.18
  513.1 150.4 %reduce-scatter.5.cloned.1.call-start = ((), (), s32[]{:S(2)}) async-start(), calls=%async_computation.8 | async-start | bytes 2228224 | tf_op jit(solution)/shard_map/reduce_scatter | solution.py:188
  516.0 224.3 %reduce-scatter.9.cloned.1.call-start = ((), (), s32[]{:S(2)}) async-start(), calls=%async_computation.10 | async-start | bytes 2228224 | tf_op jit(solution)/shard_map/reduce_scatter | solution.py:194
  518.4 27.3 %copy-start.16 = (s32[1,3]{1,0:T(1,128)S(1)}, s32[1,3]{1,0:T(1,128)}, u32[]{:S(2)}) copy-start(s32[1,3]{1,0:T(1,128)} %param.19) | copy-start | bytes 40
  518.4 14.0 %collective-permute-start.9 = (bf16[128,1024]{1,0:T(8,128)(2,1)S(1)}, bf16[128,1024]{1,0:T(8,128)(2,1)S(1)}, u32[]{:S(2)}, u32[]{:S(2)}) collective-permute-start(bf16[128,1024]{1,0:T(8,128)(2,1)S(1)} %get-tuple-element.275), channel_id=1, source_target_pairs={{0,16},{16,0},{32,48},{48,32},{64,80},{80,64},{96,112},{112,96},{1... | collective-permute-start | bytes 786440 | tf_op jit(solution)/shard_map/ppermute | solution.py:21
  529.5 8.0 collective-permute-start.11
  529.9 15.3 %collective-permute-start.10 = (bf16[128,1024]{1,0:T(8,128)(2,1)S(1)}, bf16[128,1024]{1,0:T(8,128)(2,1)S(1)}, u32[]{:S(2)}, u32[]{:S(2)}) collective-permute-start(bf16[128,1024]{1,0:T(8,128)(2,1)S(1)} %get-tuple-element.277), channel_id=1, source_target_pairs={{0,32},{32,0},{16,48},{48,16},{64,96},{96,64},{80,112},{112,80},{1... | collective-permute-start | bytes 786440 | tf_op jit(solution)/shard_map/ppermute | solution.py:21
  547.5 1.9 copy-start.1
  549.8 0.9 copy-start.7
  553.4 263.6 %reduce-scatter.7.cloned.1.call-start = ((), (), s32[]{:S(2)}) async-start(), calls=%async_computation.9 | async-start | bytes 2228224 | tf_op jit(solution)/shard_map/reduce_scatter | solution.py:191
  555.7 7.1 collective-permute-start.6
  559.0 8.0 collective-permute-start.8
  559.9 19.2 %collective-permute-start.7 = (bf16[128,1024]{1,0:T(8,128)(2,1)S(1)}, bf16[128,1024]{1,0:T(8,128)(2,1)S(1)}, u32[]{:S(2)}, u32[]{:S(2)}) collective-permute-start(bf16[128,1024]{1,0:T(8,128)(2,1)S(1)} %get-tuple-element.280), channel_id=1, source_target_pairs={{0,32},{32,0},{16,48},{48,16},{64,96},{96,64},{80,112},{112,80},{1... | collective-permute-start | bytes 786440 | tf_op jit(solution)/shard_map/ppermute | solution.py:21
  581.3 1.9 copy-start.2
  587.2 1.1 copy-start.6
  587.2 386.3 %all-reduce.3.cloned.1.call-start = ((), (), s32[]{:S(2)}) async-start(), calls=%async_computation.12 | async-start | bytes 1048576 | tf_op jit(solution)/shard_map/psum | solution.py:202
  588.3 3.6 copy-start.20
  592.0 1.1 copy-start.12
  592.0 1.8 copy-start.19
  593.8 1.1 copy-start.8
  593.8 1.8 copy-start.9
  595.7 221.3 %copy-start.13 = (f32[384]{0:T(512)S(1)}, f32[384]{0:T(512)}, u32[]{:S(2)}) copy-start(f32[384]{0:T(512)} %get-tuple-element.287) | copy-start | bytes 4612
  (1 other events, 0.9 us)
Sparse Core Ops, SparseCore 0:
  9.8 67.6 all-gather.4
  79.3 71.2 all-gather.8
  152.3 70.7 all-gather.6
  224.8 71.3 all-gather.10
  513.2 77.0 reduce-scatter.10
  592.7 70.7 reduce-scatter.4
  666.0 74.2 reduce-scatter.8
  742.9 74.0 reduce-scatter.6
  819.8 153.7 all-reduce.2
where the time goes:
time: 994 us; the launch traced here: 987 us
  waiting for transfers between devices  647 us (65%)
  matrix products  202 us (20%)
  local copies, waits for them, and re-layouts  51.3 us (5%)
  starting transfers between devices  49.4 us (5%)
  other arithmetic  20 us (2%)
  between operations  16.3 us (2%)
    psum x1, waiting for transfers between devices, local(): lax.psum(shards[0].astype(jnp.bfloat16), 'face').astype(jnp.float32)  155 us
    reduce_scatter x1, waiting for transfers between devices, local(): lax.psum_scatter(terms[2].astype(jnp.bfloat16), 'fsdp', scatter_dimension...  76.8 us
    reduce_scatter x1, waiting for transfers between devices, local(): lax.psum_scatter(terms[1].astype(jnp.bfloat16), 'fsdp', scatter_dimension...  76.6 us
    all_gather x1, waiting for transfers between devices, local(): full_out = lax.all_gather(out_weight, 'fsdp', axis=0, tiled=True)  66.8 us
    reduce_scatter x1, waiting for transfers between devices, local(): lax.psum_scatter(terms[0].astype(jnp.bfloat16), 'fsdp', scatter_dimension...  66.5 us
    all_gather x1, waiting for transfers between devices, local(): lax.all_gather(value_weight, 'fsdp', axis=0, tiled=True)  61.3 us
    dot_general x4, matrix products, head_step(): jnp.einsum('hij,jhd->ihd', grad_scores, key_part, preferred_element_type=...  60.1 us
    all_gather x1, waiting for transfers between devices, local(): lax.all_gather(query_weight, 'fsdp', axis=0, tiled=True)  57.9 us
  transfers between devices with their start and end apart: 21, of which 12 were waited for; matrix products, arithmetic and copies ran while one was open for 5% of the time, Pallas kernels for 0%

commit v1 on v0

v1 whole, which is shorter than its diff:
```python
import functools

import jax
import jax.numpy as jnp
from jax import lax
from jax.experimental import pallas as pl
from jax.experimental.pallas import tpu as pltpu
from jax.sharding import Mesh, PartitionSpec as P


TILE = 128
TILES = 3
ROWS = TILE * TILES
PAIR_ROWS = 2 * ROWS
HEAD = 64
HALF = 512
PIECE = 128
epsilon = 1e-06

FACE = ("y", "xh", "core")
PLANE = ("y", "xh")
FSDP = ("z", "xl")
NODES = FACE + FSDP
SWAP = [(0, 1), (1, 0)]


def contract_rows(left, right):
    return lax.dot_general(
        left, right, (((0,), (0,)), ((), ())), preferred_element_type=jnp.float32
    )


def times_transpose(left, right):
    return lax.dot_general(
        left, right, (((1,), (1,)), ((), ())), preferred_element_type=jnp.float32
    )


def dot(left, right):
    return jnp.dot(left, right, preferred_element_type=jnp.float32)


def swap_core(value):
    return lax.ppermute(value, "core", SWAP)


def ordered(mine, theirs, core, axis):
    size = mine.shape[axis]
    three = jnp.concatenate([theirs, mine, theirs], axis=axis)
    return lax.dynamic_slice_in_dim(three, (1 - core) * size, 2 * size, axis)


def attention_kernel(
    mask_ref, ids_ref, q_ref, k_ref, v_ref, g_ref, k1_ref, v1_ref, k2_ref, v2_ref,
    out_ref, gq_ref, gk_ref, gv_ref, bk_ref, bv_ref, score_ref, grad_ref,
):
    lane = lax.broadcasted_iota(jnp.int32, (1, 2 * HEAD), 1)
    column = lax.broadcasted_iota(jnp.int32, (1, ROWS), 1)
    sides = [(lane < HEAD), (lane >= HEAD)]
    zero = jnp.zeros((), jnp.bfloat16)
    border_k, border_v = [], []
    for block in range(2):
        rows = pl.ds(block * ROWS, ROWS)
        other = pl.ds(
            pl.multiple_of((1 - block) * ROWS + ids_ref[1 - block, 0] * TILE, TILE), TILE
        )
        keys = jnp.concatenate([k_ref[rows, :], k_ref[other, :], k1_ref[block], k2_ref[block]], 0)
        values = jnp.concatenate([v_ref[rows, :], v_ref[other, :], v1_ref[block], v2_ref[block]], 0)
        queries = q_ref[rows, :]
        grads = g_ref[rows, :]
        biases = []
        for slot in range(2 * TILES):
            parts = [mask_ref[block * TILES + t, slot] for t in range(TILES)]
            live = jnp.where(
                column < TILE, parts[0], jnp.where(column < 2 * TILE, parts[1], parts[2])
            )
            biases.append(jnp.where(live > 0, 0.0, -1e30).astype(jnp.float32))
        out = gq = gk = gv = None
        for side in sides:
            q_side = jnp.where(side, queries * jnp.bfloat16(0.125), zero)
            g_side = jnp.where(side, grads, zero)
            k_side = jnp.where(side, keys * jnp.bfloat16(0.125), zero)
            v_side = jnp.where(side, values, zero)
            top = None
            for slot in range(2 * TILES):
                span = slice(slot * TILE, (slot + 1) * TILE)
                score = times_transpose(keys[span], q_side) + biases[slot]
                score_ref[span, :] = score
                peak = jnp.max(score, axis=0, keepdims=True)
                top = peak if top is None else jnp.maximum(top, peak)
            total = inner = None
            for slot in range(2 * TILES):
                span = slice(slot * TILE, (slot + 1) * TILE)
                expo = jnp.exp(score_ref[span, :] - top)
                grad = times_transpose(values[span], g_side)
                score_ref[span, :] = expo
                grad_ref[span, :] = grad
                part = jnp.sum(expo, axis=0, keepdims=True)
                cross = jnp.sum(expo * grad, axis=0, keepdims=True)
                total = part if total is None else total + part
                inner = cross if inner is None else inner + cross
            scale = 1.0 / total
            inner = inner * scale
            probs, slopes = [], []
            for slot in range(2 * TILES):
                span = slice(slot * TILE, (slot + 1) * TILE)
                weight = score_ref[span, :] * scale
                probs.append(weight.astype(jnp.bfloat16))
                slopes.append((weight * (grad_ref[span, :] - inner)).astype(jnp.bfloat16))
            probs = jnp.concatenate(probs, 0)
            slopes = jnp.concatenate(slopes, 0)
            parts = (
                contract_rows(v_side, probs),
                contract_rows(k_side, slopes),
                dot(slopes, q_side),
                dot(probs, g_side),
            )
            if out is None:
                out, gq, gk, gv = parts
            else:
                out, gq, gk, gv = out + parts[0], gq + parts[1], gk + parts[2], gv + parts[3]
        out_ref[rows, :] = out.T.astype(jnp.bfloat16)
        gq_ref[rows, :] = gq.T.astype(jnp.bfloat16)
        gk_ref[rows, :] = gk[:ROWS]
        gv_ref[rows, :] = gv[:ROWS]
        border_k.append(gk[ROWS : ROWS + TILE].astype(jnp.bfloat16))
        border_v.append(gv[ROWS : ROWS + TILE].astype(jnp.bfloat16))
        for slot in range(2):
            span = slice(ROWS + (slot + 1) * TILE, ROWS + (slot + 2) * TILE)
            bk_ref[slot, block] = gk[span].astype(jnp.bfloat16)
            bv_ref[slot, block] = gv[span].astype(jnp.bfloat16)
    for block in range(2):
        other = pl.ds(
            pl.multiple_of((1 - block) * ROWS + ids_ref[1 - block, 0] * TILE, TILE), TILE
        )
        gk_ref[other, :] += border_k[block].astype(jnp.float32)
        gv_ref[other, :] += border_v[block].astype(jnp.float32)


def attention(mask, ids, q, kv, g, border1, border2):
    pair = 2 * HEAD
    steps = HALF // pair

    def flat(shift):
        return pl.BlockSpec((PAIR_ROWS, pair), lambda j: (0, j + shift))

    def tile(shift):
        return pl.BlockSpec((2, TILE, pair), lambda j: (0, 0, j + shift))

    smem = pl.BlockSpec(memory_space=pltpu.SMEM)
    border = pl.BlockSpec((2, 2, TILE, pair), lambda j: (0, 0, 0, j))
    return pl.pallas_call(
        attention_kernel,
        grid=(steps,),
        in_specs=[
            smem, smem, flat(0), flat(0), flat(steps), flat(0),
            tile(0), tile(steps), tile(0), tile(steps),
        ],
        out_specs=[flat(0), flat(0), flat(0), flat(0), border, border],
        out_shape=[
            jax.ShapeDtypeStruct((PAIR_ROWS, HALF), jnp.bfloat16),
            jax.ShapeDtypeStruct((PAIR_ROWS, HALF), jnp.bfloat16),
            jax.ShapeDtypeStruct((PAIR_ROWS, HALF), jnp.float32),
            jax.ShapeDtypeStruct((PAIR_ROWS, HALF), jnp.float32),
            jax.ShapeDtypeStruct((2, 2, TILE, HALF), jnp.bfloat16),
            jax.ShapeDtypeStruct((2, 2, TILE, HALF), jnp.bfloat16),
        ],
        scratch_shapes=[
            pltpu.VMEM((2 * ROWS, ROWS), jnp.float32),
            pltpu.VMEM((2 * ROWS, ROWS), jnp.float32),
        ],
        compiler_params=pltpu.CompilerParams(vmem_limit_bytes=40 * 1024 * 1024),
        cost_estimate=pl.CostEstimate(
            flops=15_000_000_000, bytes_accessed=16_000_000, transcendentals=5_000_000
        ),
        name="attention",
    )(mask, ids, q, kv, kv, g, border1, border1, border2, border2)


def spread(value, axes, count):
    copies = jnp.broadcast_to(value[None], (count,) + value.shape)
    return lax.all_to_all(copies, axes, 0, 0, tiled=True)


def norm(features, gain):
    wide = features.astype(jnp.float32)
    inverse = lax.rsqrt(jnp.mean(wide * wide, axis=1, keepdims=True) + epsilon)
    return wide, inverse, (wide * inverse * gain).astype(jnp.bfloat16)


def reduce_half(term, sums):
    pieces = term.astype(jnp.bfloat16).reshape(1024, 8, PIECE).transpose(1, 0, 2)
    arrived = lax.all_to_all(pieces, PLANE, 0, 0, tiled=True)
    part = jnp.sum(arrived.astype(jnp.float32), axis=0).astype(jnp.bfloat16)
    arrived = lax.all_to_all(part.reshape(16, 64, PIECE), FSDP, 0, 0, tiled=True)
    return jnp.sum(arrived.astype(jnp.float32), axis=0).astype(jnp.bfloat16)


def local(
    node_features, norm_gain, query_weight, key_weight, value_weight, out_weight,
    cotangent, pair_mask, border_ids,
):
    core = lax.axis_index("core")
    plane = lax.axis_index("y") * 2 + lax.axis_index("xh")

    def half_of(value, which):
        return lax.dynamic_slice_in_dim(value, which * HALF, HALF, 1)

    first = jnp.concatenate([half_of(key_weight, core), half_of(value_weight, core)], 1)
    second = jnp.concatenate([half_of(query_weight, core), half_of(out_weight, core)], 1)
    piece = lax.dynamic_slice_in_dim(jnp.stack([first, second]), plane * PIECE, PIECE, 2)
    fetched = spread(piece, FSDP, 16)
    first_piece = fetched[:, 0].reshape(1024, PIECE)
    second_piece = fetched[:, 1].reshape(1024, PIECE)
    key_value = spread(first_piece, PLANE, 8).transpose(1, 0, 2).reshape(1024, 1024)

    features = ordered(node_features, swap_core(node_features), core, 0)
    cotangent_half = ordered(
        half_of(cotangent, core), swap_core(half_of(cotangent, 1 - core)), core, 0
    )
    plan = jnp.concatenate([pair_mask, jnp.broadcast_to(border_ids, (TILES, TILES))], 1)
    plan = ordered(plan, swap_core(plan), core, 0)
    mask = plan[:, : 2 * TILES]
    ids = plan[:: TILES, 2 * TILES :]

    normed = norm(features, norm_gain)[2]
    kv = dot(normed, key_value).astype(jnp.bfloat16)
    arrived = []
    for bit, (axis, route) in ((1, ("xh", SWAP)), (2, ("y", [(0, 1), (1, 0), (2, 3), (3, 2)]))):
        sent = jnp.stack(
            [
                lax.dynamic_slice_in_dim(kv, block * ROWS + ids[block, bit] * TILE, TILE, 0)
                for block in range(2)
            ]
        )
        arrived.append(lax.ppermute(sent, axis, route))

    query_out = spread(second_piece, PLANE, 8).transpose(1, 0, 2).reshape(1024, 1024)
    query_half, out_half = query_out[:, :HALF], query_out[:, HALF:]
    q = dot(normed, query_half).astype(jnp.bfloat16)
    grad_part = times_transpose(cotangent_half, out_half)
    grad_attended = (
        half_of(grad_part, core) + swap_core(half_of(grad_part, 1 - core))
    ).astype(jnp.bfloat16)

    attended, grad_q, own_k, own_v, back_k, back_v = attention(
        mask, ids, q, kv, grad_attended, arrived[0], arrived[1]
    )
    returned = []
    for slot, (axis, route) in enumerate((("xh", SWAP), ("y", [(0, 1), (1, 0), (2, 3), (3, 2)]))):
        returned.append(lax.ppermute(jnp.stack([back_k[slot], back_v[slot]]), axis, route))

    attended_all = ordered(attended, swap_core(attended), core, 1)
    update = dot(attended_all, out_half).astype(jnp.bfloat16)
    update_mine = lax.dynamic_slice_in_dim(update, core * ROWS, ROWS, 0)
    update_theirs = lax.dynamic_slice_in_dim(update, (1 - core) * ROWS, ROWS, 0)
    layer_update = ordered(update_mine, swap_core(update_theirs), core, 1)

    term_second = jnp.concatenate(
        [contract_rows(normed, grad_q), contract_rows(attended_all, cotangent_half)], 1
    )
    sum_second = reduce_half(term_second, None)

    selector = (ids[:, 1:, None] == jnp.arange(TILES, dtype=jnp.int32)).astype(jnp.float32)
    extra = sum(
        selector[:, slot, :, None, None].reshape(1, 2, TILES, 1, 1)
        * returned[slot].astype(jnp.float32)[:, :, None]
        for slot in range(2)
    ).reshape(2, PAIR_ROWS, HALF)
    grad_k = (own_k + extra[0]).astype(jnp.bfloat16)
    grad_v = (own_v + extra[1]).astype(jnp.bfloat16)
    grad_kv = jnp.concatenate([grad_k, grad_v], 1)
    sum_first = reduce_half(contract_rows(normed, grad_kv), None)

    grad_normed = times_transpose(grad_q, query_half) + times_transpose(grad_kv, key_value)
    grad_mine = lax.dynamic_slice_in_dim(grad_normed, core * ROWS, ROWS, 0)
    grad_theirs = lax.dynamic_slice_in_dim(grad_normed, (1 - core) * ROWS, ROWS, 0)
    scaled = (grad_mine + swap_core(grad_theirs)) * norm_gain
    wide, inverse, _ = norm(node_features, norm_gain)
    inner_mean = jnp.mean(scaled * wide, axis=1, keepdims=True)
    node_gradient = (inverse * scaled - wide * inverse**3 * inner_mean).astype(jnp.bfloat16)

    gathered = spread(jnp.stack([sum_first, sum_second]), FACE, 16)
    gathered = gathered.reshape(2, 4, 2, 2, 64, PIECE)
    gathered = gathered.transpose(3, 0, 4, 2, 1, 5).reshape(2, 2, 64, 1024).astype(jnp.float32)
    return (
        layer_update, node_gradient, gathered[1, 0], gathered[0, 0], gathered[0, 1], gathered[1, 1]
    )


def solution(mesh):
    fine = Mesh(mesh.devices.reshape(4, 2, 2, 8, 2), NODES)
    rows = P(NODES, None)
    weight = P(FSDP, None)
    return jax.shard_map(
        local,
        mesh=fine,
        in_specs=(rows, P(), weight, weight, weight, weight, rows, rows, rows),
        out_specs=(rows, rows, weight, weight, weight, weight),
        check_vma=False,
    )
```

time: 994 us -> 283 us (0.28)
  waiting for transfers between devices: 647 us -> 88.9 us
  matrix products: 202 us -> 21.3 us
  local copies, waits for them, and re-layouts: 51.3 us -> 20.1 us
  blocking collectives: 0 us -> 25.5 us
  Pallas kernels: 0 us -> 24.3 us
  starting transfers between devices: 49.4 us -> 67.2 us
  between operations: 16.3 us -> 3.78 us
  other arithmetic: 20 us -> 30.8 us
    all_gather x4 -> x0, waiting for transfers between devices: 241 us -> none  [the longest x1 66.8 us: local(): full_out = lax.all_gather(out_weight, 'fsdp', axis=0, tiled=True)]
    reduce_scatter x4 -> x0, waiting for transfers between devices: 220 us -> none  [the longest x1 76.8 us: local(): lax.psum_scatter(terms[2].astype(jnp.bfloat16), 'fsdp', scatter_dimension...]
    dot_general x26 -> x3, matrix products: 166 us -> 8.23 us  [dot(): return jnp.dot(left, right, preferred_element_type=jnp.float32)]
    psum x1 -> x0, waiting for transfers between devices: 155 us -> none  [local(): lax.psum(shards[0].astype(jnp.bfloat16), 'face').astype(jnp.float32)]
    all_to_all x0 -> x7, waiting for transfers between devices: none -> 68.8 us  [the longest x3 41.1 us: spread(): return lax.all_to_all(copies, axes, 0, 0, tiled=True)]
    all_to_all x0 -> x7, starting transfers between devices: none -> 44.7 us  [the longest x3 21.3 us: spread(): return lax.all_to_all(copies, axes, 0, 0, tiled=True)]
    ppermute x12 -> x11, starting transfers between devices: 48.8 us -> 22.5 us  [the longest x7 14.5 us: swap_core(): return lax.ppermute(value, 'core', SWAP)]
    all_to_all x0 -> x1, blocking collectives: none -> 25.5 us  [spread(): return lax.all_to_all(copies, axes, 0, 0, tiled=True)]
  transfers between devices with their start and end apart: 21 -> 18, of which waited for: 12 -> 13; matrix products, arithmetic and copies ran while one was open for 5% -> 18% of each run, Pallas kernels for 0% -> 0%
where the time goes in v1:
time: 283 us; the launch traced here: 282 us
  waiting for transfers between devices  88.9 us (31%)
  starting transfers between devices  67.2 us (24%)
  other arithmetic  30.8 us (11%)
  blocking collectives  25.5 us (9%)
  Pallas kernels  24.3 us (9%)
  matrix products  21.3 us (8%)
  local copies, waits for them, and re-layouts  20.1 us (7%)
  between operations  3.78 us (1%)
    all_to_all x3, waiting for transfers between devices, spread(): return lax.all_to_all(copies, axes, 0, 0, tiled=True)  41.1 us
    all_to_all x1, blocking collectives, spread(): return lax.all_to_all(copies, axes, 0, 0, tiled=True)  25.5 us
    pallas_call x1, Pallas kernels, attention(): pl.pallas_call(attention_kernel, grid=(steps,), in_specs=[smem, smem, fla...  24.3 us
    all_to_all x2, waiting for transfers between devices, reduce_half(): arrived = lax.all_to_all(pieces, PLANE, 0, 0, tiled=True)  23.9 us
    all_to_all x3, starting transfers between devices, spread(): return lax.all_to_all(copies, axes, 0, 0, tiled=True)  21.3 us
    ppermute x7, starting transfers between devices, swap_core(): return lax.ppermute(value, 'core', SWAP)  14.5 us
    all_to_all x2, starting transfers between devices, reduce_half(): lax.all_to_all(part.reshape(16, 64, PIECE), FSDP, 0, 0, tiled=True)  12.5 us
    all_to_all x2, starting transfers between devices, reduce_half(): arrived = lax.all_to_all(pieces, PLANE, 0, 0, tiled=True)  10.9 us
  transfers between devices with their start and end apart: 18, of which 13 were waited for; matrix products, arithmetic and copies ran while one was open for 18% of the time, Pallas kernels for 0%

profile of v1, /device:TPU:1, one launch (start us, length us, event | category | flops | bytes accessed | tf_op | source)
XLA Modules:
  0.0 281.9 jit_solution(15983711420765820785)
XLA Ops:
  2.6 25.5 %all_to_all.40 = bf16[16,2,64,128]{3,2,1,0:T(8,128)(2,1)S(1)} all-to-all(bf16[16,2,64,128]{3,2,1,0:T(8,128)(2,1)S(1)} %broadcast_in_dim.18), channel_id=1, replica_groups=mesh['y'=4,'xh'=2,'core'=2,'z'=8,'xl'=2] {'z','xl'}, dimensions={0} | all-to-all | bytes 1048576 | tf_op jit(solution)/shard_map/all_to_all | solution.py:182
  28.3 1.6 broadcast_in_dim.20
  29.9 6.4 %all-to-all-start.1 = ((bf16[8,1024,128]{1,2,0:T(8,128)(2,1)}), bf16[8,1024,128]{1,2,0:T(8,128)(2,1)S(1)}, u32[]{:S(2)}, u32[]{:S(2)}) async-start(bf16[8,1024,128]{1,2,0:T(8,128)(2,1)} %broadcast_in_dim.20), calls=%async_computation.1 | async-start | bytes 4194304 | tf_op jit(solution)/shard_map/all_to_all | solution.py:182
  36.4 25.3 %all-to-all-done.1 = bf16[8,1024,128]{1,2,0:T(8,128)(2,1)S(1)} async-done(((bf16[8,1024,128]{1,2,0:T(8,128)(2,1)}), bf16[8,1024,128]{1,2,0:T(8,128)(2,1)S(1)}, u32[]{:S(2)}, u32[]{:S(2)}) %all-to-all-start.1) | async-done | bytes 2097184 | tf_op jit(solution)/shard_map/all_to_all | solution.py:182
  61.7 1.8 broadcast_in_dim.22
  63.6 5.7 %all-to-all-start.2 = ((bf16[8,1024,128]{1,2,0:T(8,128)(2,1)}), bf16[8,1024,128]{1,2,0:T(8,128)(2,1)}, u32[]{:S(2)}, u32[]{:S(2)}) async-start(bf16[8,1024,128]{1,2,0:T(8,128)(2,1)} %broadcast_in_dim.22), calls=%async_computation.2 | async-start | bytes 4194304 | tf_op jit(solution)/shard_map/all_to_all | solution.py:182
  69.4 2.9 %collective-permute-start.2 = (bf16[384,512]{1,0:T(8,128)(2,1)S(1)}, bf16[384,512]{1,0:T(8,128)(2,1)S(1)}, u32[]{:S(2)}, u32[]{:S(2)}) collective-permute-start(bf16[384,512]{1,0:T(8,128)(2,1)S(1)} %get-tuple-element.65), channel_id=1, source_target_pairs={{0,16},{16,0},{1,17},{17,1},{2,18},{18,2},{3,19},{19,3},{4,20},{20... | collective-permute-start | bytes 1179656 | tf_op jit(solution)/shard_map/ppermute | solution.py:44
  72.9 1.9 collective-permute-done
  78.2 1.7 fusion.23
  79.8 2.5 fusion.16
  82.3 1.3 constant_dynamic-slice_fusion.6
  84.0 3.5 %fusion = (f32[768]{0:T(1024)S(1)}, bf16[768,1024]{1,0:T(8,128)(2,1)}) fusion(s32[]{:T(128)S(6)} %select_n.47, bf16[384,1024]{1,0:T(8,128)(2,1)} %collective-permute-done.1, bf16[384,1024]{1,0:T(8,128)(2,1)} %param.9), kind=kLoop, calls=%fused_computation.2 | loop fusion | flops 7077120 | bytes 3148804 | tf_op jit(solution)/shard_map/reduce_sum | solution.py:187
  87.5 7.3 %all-to-all-done.2 = bf16[8,1024,128]{1,2,0:T(8,128)(2,1)} async-done(((bf16[8,1024,128]{1,2,0:T(8,128)(2,1)}), bf16[8,1024,128]{1,2,0:T(8,128)(2,1)}, u32[]{:S(2)}, u32[]{:S(2)}) %all-to-all-start.2) | async-done | bytes 2097184 | tf_op jit(solution)/shard_map/all_to_all | solution.py:182
  94.9 3.9 %convolution_convert_fusion.1.k_ref.v_ref = bf16[768,1024]{1,0:T(8,128)(2,1)S(1)} fusion(bf16[1024,1024]{0,1:T(8,128)(2,1)} %bitcast.8, bf16[768,1024]{1,0:T(8,128)(2,1)} %get-tuple-element.51, f32[1024]{0:T(1024)S(1)} %copy-done.21, f32[768]{0:T(1024)S(1)} %add_rsqrt_fusion), kind=kOutput, calls=%fused_computation.18 | convolution fusion | flops 1614544896 | bytes 5250048 | tf_op jit(solution)/shard_map/dot_general | solution.py:40
  99.1 4.2 %collective-permute-start.4 = (bf16[2,128,1024]{2,1,0:T(8,128)(2,1)S(1)}, bf16[2,128,1024]{2,1,0:T(8,128)(2,1)S(1)}, u32[]{:S(2)}, u32[]{:S(2)}) collective-permute-start(bf16[2,128,1024]{2,1,0:T(8,128)(2,1)S(1)} %pad_maximum_fusion.3), channel_id=1, source_target_pairs={{0,32},{32,0},{1,33},{33,1},{2,34},{34,2},{3,35},{35,3},{4,36},{36... | collective-permute-start | bytes 1572872 | tf_op jit(solution)/shard_map/ppermute | solution.py:236
  104.4 1.7 add_convert_fusion.g_ref
  106.0 2.5 collective-permute-done.5.k2_ref.v2_ref
  108.5 4.9 %collective-permute-done.4.k1_ref.v1_ref = bf16[2,128,1024]{2,1,0:T(8,128)(2,1)S(1)} collective-permute-done((bf16[2,128,1024]{2,1,0:T(8,128)(2,1)S(1)}, bf16[2,128,1024]{2,1,0:T(8,128)(2,1)S(1)}, u32[]{:S(2)}, u32[]{:S(2)}) %collective-permute-start.4) | collective-permute-done | bytes 524320 | tf_op jit(solution)/shard_map/ppermute | solution.py:236
  113.4 24.3 %attention.1 = (bf16[768,512]{1,0:T(8,128)(2,1)S(1)}, bf16[768,512]{1,0:T(8,128)(2,1)S(1)}, f32[768,512]{1,0:T(8,128)S(1)}, f32[768,512]{1,0:T(8,128)S(1)}, bf16...) custom-call(s32[6,6]{1,0:T(8,128)S(1)} %bitcast.75, s32[2,3]{1,0:T(2,128)S(1)} %slice.72.ids_ref, ...), custom_call_target="tpu_custom_call" | custom-call | flops 15000000512 | bytes 16000000 | tf_op jit(solution)/shard_map/attention/pallas_call | solution.py:152
  139.1 3.7 %collective-permute-start.8 = (bf16[2,2,128,512]{3,2,1,0:T(8,128)(2,1)}, bf16[2,2,128,512]{3,2,1,0:T(8,128)(2,1)}, u32[]{:S(2)}, u32[]{:S(2)}) collective-permute-start(bf16[2,2,128,512]{3,2,1,0:T(8,128)(2,1)} %pad_maximum_fusion.5), channel_id=1, source_target_pairs={{0,32},{32,0},{1,33},{33,1},{2,34},{34,2},{3,35},{35,3},{4,36},{36... | collective-permute-start | bytes 1572872 | tf_op jit(solution)/shard_map/ppermute | solution.py:251
  143.9 9.2 %collective-permute-done.8 = bf16[2,2,128,512]{3,2,1,0:T(8,128)(2,1)} collective-permute-done((bf16[2,2,128,512]{3,2,1,0:T(8,128)(2,1)}, bf16[2,2,128,512]{3,2,1,0:T(8,128)(2,1)}, u32[]{:S(2)}, u32[]{:S(2)}) %collective-permute-start.8) | collective-permute-done | bytes 524320 | tf_op jit(solution)/shard_map/ppermute | solution.py:251
  153.0 1.2 convert_element_type.72
  159.2 3.4 %convolution_convert_fusion = bf16[1024,1024]{0,1:T(8,128)(2,1)} fusion(bf16[768,512]{1,0:T(8,128)(2,1)S(1)} %fusion.12, bf16[768,512]{1,0:T(8,128)(2,1)S(1)} %fusion.13, bf16[768,1024]{1,0:T(8,128)(2,1)S(1)} %copy-done.12, f32[1024]{0:T(1024)S(1)} %copy-done.21, f32[768]{0:T(1024)S(1)} %add_rsqrt_fusion), kind=kOutput, calls=%fused_computation.17 | convolution fusion | flops 1617952768 | bytes 5250048 | tf_op jit(solution)/shard_map/dot_general | solution.py:28
  162.6 5.3 %all-to-all-start.3 = ((bf16[8,1024,128]{1,2,0:T(8,128)(2,1)}), bf16[8,1024,128]{1,2,0:T(8,128)(2,1)}, u32[]{:S(2)}, u32[]{:S(2)}) async-start(bf16[8,1024,128]{1,2,0:T(8,128)(2,1)} %bitcast.80), calls=%async_computation.3 | async-start | bytes 4194304 | tf_op jit(solution)/shard_map/all_to_all | solution.py:193
  167.9 3.2 %collective-permute-start.6 = (bf16[768,512]{1,0:T(8,128)(2,1)S(1)}, bf16[768,512]{1,0:T(8,128)(2,1)}, u32[]{:S(2)}, u32[]{:S(2)}) collective-permute-start(bf16[768,512]{1,0:T(8,128)(2,1)S(1)} %copy-done.1), channel_id=1, source_target_pairs={{0,16},{16,0},{1,17},{17,1},{2,18},{18,2},{3,19},{19,3},{4,20},{20... | collective-permute-start | bytes 2359304 | tf_op jit(solution)/shard_map/ppermute | solution.py:44
  171.1 1.2 convolution_convert_fusion.3
  173.2 2.0 fusion.4
  176.3 1.6 maximum_bitcast_fusion
  177.9 15.2 %all-to-all-done.3 = bf16[8,1024,128]{1,2,0:T(8,128)(2,1)} async-done(((bf16[8,1024,128]{1,2,0:T(8,128)(2,1)}), bf16[8,1024,128]{1,2,0:T(8,128)(2,1)}, u32[]{:S(2)}, u32[]{:S(2)}) %all-to-all-start.3) | async-done | bytes 2097184 | tf_op jit(solution)/shard_map/all_to_all | solution.py:193
  193.1 5.6 %all-to-all-start.5 = ((bf16[8,1024,128]{1,2,0:T(8,128)(2,1)}), bf16[8,1024,128]{1,2,0:T(8,128)(2,1)}, u32[]{:S(2)}, u32[]{:S(2)}) async-start(bf16[8,1024,128]{1,2,0:T(8,128)(2,1)} %maximum_bitcast_fusion), calls=%async_computation.5 | async-start | bytes 4194304 | tf_op jit(solution)/shard_map/all_to_all | solution.py:193
  198.6 4.0 %fusion.14 = f32[768,1024]{1,0:T(8,128)S(1)} fusion(bf16[1024,1024]{0,1:T(8,128)(2,1)} %bitcast.8, bf16[768,512]{1,0:T(8,128)(2,1)} %copy-done.19, bf16[768,512]{1,0:T(8,128)(2,1)} %copy-done.18), kind=kOutput, calls=%fused_computation.46 | convolution fusion | flops 1613758464 | bytes 6815744 | tf_op jit(solution)/shard_map/dot_general | solution.py:34
  203.7 1.4 constant_dynamic-slice_fusion.3
  205.8 3.1 %collective-permute-start.10 = (f32[384,1024]{1,0:T(8,128)}, f32[384,1024]{1,0:T(8,128)}, u32[]{:S(2)}, u32[]{:S(2)}) collective-permute-start(f32[384,1024]{1,0:T(8,128)} %constant_dynamic-slice_fusion.3), channel_id=1, source_target_pairs={{0,16},{16,0},{1,17},{17,1},{2,18},{18,2},{3,19},{19,3},{4,20},{20... | collective-permute-start | bytes 4718600 | tf_op jit(solution)/shard_map/ppermute | solution.py:44
  209.0 3.3 %convolution_convert_fusion.4 = bf16[768,512]{0,1:T(8,128)(2,1)} fusion(bf16[768,1024]{1,0:T(8,128)(2,1)} %copy-done.13, bf16[1024,1024]{0,1:T(8,128)(2,1)S(1)} %bitcast.79), kind=kOutput, calls=%fused_computation.37 | convolution fusion | flops 805699584 | bytes 3407872 | tf_op jit(solution)/shard_map/dot_general | solution.py:40
  212.3 2.0 reduce_sum.78
  215.2 8.7 %all-to-all-done.5 = bf16[8,1024,128]{1,2,0:T(8,128)(2,1)} async-done(((bf16[8,1024,128]{1,2,0:T(8,128)(2,1)}), bf16[8,1024,128]{1,2,0:T(8,128)(2,1)}, u32[]{:S(2)}, u32[]{:S(2)}) %all-to-all-start.5) | async-done | bytes 2097184 | tf_op jit(solution)/shard_map/all_to_all | solution.py:193
  223.8 7.0 %all-to-all-start.4 = ((bf16[16,64,128]{2,1,0:T(8,128)(2,1)}), bf16[16,64,128]{2,1,0:T(8,128)(2,1)S(1)}, u32[]{:S(2)}, u32[]{:S(2)}) async-start(bf16[16,64,128]{2,1,0:T(8,128)(2,1)} %bitcast.27), calls=%async_computation.4 | async-start | bytes 524288 | tf_op jit(solution)/shard_map/all_to_all | solution.py:195
  231.0 4.4 %collective-permute-start.7 = (bf16[384,512]{0,1:T(8,128)(2,1)S(1)}, bf16[384,512]{0,1:T(8,128)(2,1)S(1)}, u32[]{:S(2)}, u32[]{:S(2)}) collective-permute-start(bf16[384,512]{0,1:T(8,128)(2,1)S(1)} %get-tuple-element.63), channel_id=1, source_target_pairs={{0,16},{16,0},{1,17},{17,1},{2,18},{18,2},{3,19},{19,3},{4,20},{20... | collective-permute-start | bytes 1179656 | tf_op jit(solution)/shard_map/ppermute | solution.py:44
  235.4 2.0 reduce_sum.80
  238.2 2.4 all-to-all-done.4
  240.6 5.5 %all-to-all-start.6 = ((bf16[16,64,128]{2,1,0:T(8,128)(2,1)}), bf16[16,64,128]{2,1,0:T(8,128)(2,1)}, u32[]{:S(2)}, u32[]{:S(2)}) async-start(bf16[16,64,128]{2,1,0:T(8,128)(2,1)} %bitcast.32), calls=%async_computation.6 | async-start | bytes 524288 | tf_op jit(solution)/shard_map/all_to_all | solution.py:195
  246.9 3.2 %fusion.21 = bf16[384,1024]{0,1:T(8,128)(2,1)} fusion(s32[]{:T(128)S(6)} %select_n.55, bf16[384,512]{0,1:T(8,128)(2,1)} %copy-done.20, bf16[384,512]{0,1:T(8,128)(2,1)S(1)} %get-tuple-element.62), kind=kLoop, calls=%fused_computation.53 | loop fusion | flops 2359296 | bytes 1572868 | tf_op jit(solution)/shard_map/concatenate | solution.py:49
  250.0 2.3 copy.40
  252.3 2.1 fusion.7
  254.5 1.4 all-to-all-done.6
  257.9 9.2 %all-to-all-start.7 = ((bf16[16,2,64,128]{3,2,1,0:T(8,128)(2,1)}), bf16[16,2,64,128]{3,2,1,0:T(8,128)(2,1)}, u32[]{:S(2)}, u32[]{:S(2)}) async-start(bf16[16,2,64,128]{3,2,1,0:T(8,128)(2,1)} %broadcast_in_dim.23), calls=%async_computation.7 | async-start | bytes 1048576 | tf_op jit(solution)/shard_map/all_to_all | solution.py:182
  267.1 3.0 %fusion.10 = bf16[384,1024]{1,0:T(8,128)(2,1)} fusion(bf16[384,1024]{1,0:T(8,128)(2,1)} %param.9, f32[384]{0:T(512)S(1)} %broadcast_multiply_fusion, f32[384]{0:T(512)S(1)} %get-tuple-element.73, f32[384]{0:T(512)S(1)} %get-tuple-element.72, f32[1024]{0:T(1024)S(1)} %copy-done.21, f32[384,1024]{1,0:T(8,128)} %collective-permute-done.10, ...), kind=kLoop, calls=%fused_computation.26 | loop fusion | flops 3145728 | bytes 4727300 | tf_op jit(solution)/shard_map/convert_element_type | solution.py:281
  270.1 8.5 %all-to-all-done.7 = bf16[16,2,64,128]{3,2,1,0:T(8,128)(2,1)} async-done(((bf16[16,2,64,128]{3,2,1,0:T(8,128)(2,1)}), bf16[16,2,64,128]{3,2,1,0:T(8,128)(2,1)}, u32[]{:S(2)}, u32[]{:S(2)}) %all-to-all-start.7) | async-done | bytes 524320 | tf_op jit(solution)/shard_map/all_to_all | solution.py:182
  (108 shorter events, 24.5 us)
Async XLA Ops:
  29.9 31.8 %all-to-all-start.1 = ((bf16[8,1024,128]{1,2,0:T(8,128)(2,1)}), bf16[8,1024,128]{1,2,0:T(8,128)(2,1)S(1)}, u32[]{:S(2)}, u32[]{:S(2)}) async-start(bf16[8,1024,128]{1,2,0:T(8,128)(2,1)} %broadcast_in_dim.20), calls=%async_computation.1 | async-start | bytes 4194304 | tf_op jit(solution)/shard_map/all_to_all | solution.py:182
  61.7 1.9 copy-start.6
  63.5 5.8 %copy-start.16 = (bf16[384,1024]{1,0:T(8,128)(2,1)S(1)}, bf16[384,1024]{1,0:T(8,128)(2,1)}, u32[]{:S(2)}) copy-start(bf16[384,1024]{1,0:T(8,128)(2,1)} %param.15) | copy-start | bytes 2359300
  63.6 31.3 %all-to-all-start.2 = ((bf16[8,1024,128]{1,2,0:T(8,128)(2,1)}), bf16[8,1024,128]{1,2,0:T(8,128)(2,1)}, u32[]{:S(2)}, u32[]{:S(2)}) async-start(bf16[8,1024,128]{1,2,0:T(8,128)(2,1)} %broadcast_in_dim.22), calls=%async_computation.2 | async-start | bytes 4194304 | tf_op jit(solution)/shard_map/all_to_all | solution.py:182
  69.3 3.1 %copy-start.23 = (s32[1,3]{1,0:T(1,128)S(1)}, s32[1,3]{1,0:T(1,128)}, u32[]{:S(2)}) copy-start(s32[1,3]{1,0:T(1,128)} %param.17) | copy-start | bytes 40
  69.3 3.1 %copy-start.22 = (s32[3,6]{1,0:T(4,128)S(1)}, s32[3,6]{1,0:T(4,128)}, u32[]{:S(2)}) copy-start(s32[3,6]{1,0:T(4,128)} %param.16) | copy-start | bytes 220
  69.4 8.8 %collective-permute-start.2 = (bf16[384,512]{1,0:T(8,128)(2,1)S(1)}, bf16[384,512]{1,0:T(8,128)(2,1)S(1)}, u32[]{:S(2)}, u32[]{:S(2)}) collective-permute-start(bf16[384,512]{1,0:T(8,128)(2,1)S(1)} %get-tuple-element.65), channel_id=1, source_target_pairs={{0,16},{16,0},{1,17},{17,1},{2,18},{18,2},{3,19},{19,3},{4,20},{20... | collective-permute-start | bytes 1179656 | tf_op jit(solution)/shard_map/ppermute | solution.py:44
  72.3 11.7 %collective-permute-start.1 = (bf16[384,1024]{1,0:T(8,128)(2,1)}, bf16[384,1024]{1,0:T(8,128)(2,1)}, u32[]{:S(2)}, u32[]{:S(2)}) collective-permute-start(bf16[384,1024]{1,0:T(8,128)(2,1)} %param.9), channel_id=1, source_target_pairs={{0,16},{16,0},{1,17},{17,1},{2,18},{18,2},{3,19},{19,3},{4,20},{20... | collective-permute-start | bytes 2359304 | tf_op jit(solution)/shard_map/ppermute | solution.py:44
  72.5 2.3 collective-permute-start
  79.8 2.5 copy-start.9
  83.7 11.2 %copy-start.21 = (f32[1024]{0:T(1024)S(1)}, f32[1024]{0:T(1024)}, u32[]{:S(2)}) copy-start(f32[1024]{0:T(1024)} %param.10) | copy-start | bytes 12292
  83.7 20.7 %collective-permute-start.3 = (f32[768,512]{1,0:T(8,128)}, f32[768,512]{1,0:T(8,128)}, u32[]{:S(2)}, u32[]{:S(2)}) collective-permute-start(f32[768,512]{1,0:T(8,128)} %constant_dynamic-slice_fusion.6), channel_id=1, source_target_pairs={{0,16},{16,0},{1,17},{17,1},{2,18},{18,2},{3,19},{19,3},{4,20},{20... | collective-permute-start | bytes 4718600 | tf_op jit(solution)/shard_map/ppermute | solution.py:44
  98.8 4.6 %copy-start.11 = (bf16[768,1024]{1,0:T(8,128)(2,1)S(1)}, bf16[768,1024]{1,0:T(8,128)(2,1)}, u32[]{:S(2)}) copy-start(bf16[768,1024]{1,0:T(8,128)(2,1)} %get-tuple-element.51) | copy-start | bytes 4718596
  98.9 4.5 %copy-start.7 = (bf16[8,1024,128]{1,2,0:T(8,128)(2,1)S(1)}, bf16[8,1024,128]{1,2,0:T(8,128)(2,1)}, u32[]{:S(2)}) copy-start(bf16[8,1024,128]{1,2,0:T(8,128)(2,1)} %copy-done.6) | copy-start | bytes 6291460
  98.9 9.6 %collective-permute-start.5 = (bf16[2,128,1024]{2,1,0:T(8,128)(2,1)S(1)}, bf16[2,128,1024]{2,1,0:T(8,128)(2,1)S(1)}, u32[]{:S(2)}, u32[]{:S(2)}) collective-permute-start(bf16[2,128,1024]{2,1,0:T(8,128)(2,1)S(1)} %pad_maximum_fusion.4), channel_id=1, source_target_pairs={{0,64},{64,0},{128,192},{192,128},{1,65},{65,1},{129,193},{193,129... | collective-permute-start | bytes 1572872 | tf_op jit(solution)/shard_map/ppermute | solution.py:236
  99.1 14.3 %collective-permute-start.4 = (bf16[2,128,1024]{2,1,0:T(8,128)(2,1)S(1)}, bf16[2,128,1024]{2,1,0:T(8,128)(2,1)S(1)}, u32[]{:S(2)}, u32[]{:S(2)}) collective-permute-start(bf16[2,128,1024]{2,1,0:T(8,128)(2,1)S(1)} %pad_maximum_fusion.3), channel_id=1, source_target_pairs={{0,32},{32,0},{1,33},{33,1},{2,34},{34,2},{3,35},{35,3},{4,36},{36... | collective-permute-start | bytes 1572872 | tf_op jit(solution)/shard_map/ppermute | solution.py:236
  137.7 1.1 copy-start
  137.7 1.3 copy-start.2
  139.1 14.0 %collective-permute-start.8 = (bf16[2,2,128,512]{3,2,1,0:T(8,128)(2,1)}, bf16[2,2,128,512]{3,2,1,0:T(8,128)(2,1)}, u32[]{:S(2)}, u32[]{:S(2)}) collective-permute-start(bf16[2,2,128,512]{3,2,1,0:T(8,128)(2,1)} %pad_maximum_fusion.5), channel_id=1, source_target_pairs={{0,32},{32,0},{1,33},{33,1},{2,34},{34,2},{3,35},{35,3},{4,36},{36... | collective-permute-start | bytes 1572872 | tf_op jit(solution)/shard_map/ppermute | solution.py:251
  143.6 11.4 %collective-permute-start.9 = (bf16[2,2,128,512]{3,2,1,0:T(8,128)(2,1)}, bf16[2,2,128,512]{3,2,1,0:T(8,128)(2,1)}, u32[]{:S(2)}, u32[]{:S(2)}) collective-permute-start(bf16[2,2,128,512]{3,2,1,0:T(8,128)(2,1)} %pad_maximum_fusion.6), channel_id=1, source_target_pairs={{0,64},{64,0},{128,192},{192,128},{1,65},{65,1},{129,193},{193,129... | collective-permute-start | bytes 1572872 | tf_op jit(solution)/shard_map/ppermute | solution.py:251
  157.5 0.9 copy-start.18
  157.5 1.7 copy-start.12
  159.2 3.4 %copy-start.19 = (bf16[768,512]{1,0:T(8,128)(2,1)}, bf16[768,512]{1,0:T(8,128)(2,1)S(1)}, u32[]{:S(2)}) copy-start(bf16[768,512]{1,0:T(8,128)(2,1)S(1)} %fusion.12) | copy-start | bytes 2359300
  162.6 5.3 %copy-start.1 = (bf16[768,512]{1,0:T(8,128)(2,1)S(1)}, bf16[768,512]{1,0:T(8,128)(2,1)}, u32[]{:S(2)}) copy-start(bf16[768,512]{1,0:T(8,128)(2,1)} %copy-done) | copy-start | bytes 2359300
  162.6 8.5 %copy-start.3 = (bf16[768,512]{1,0:T(8,128)(2,1)S(1)}, bf16[768,512]{1,0:T(8,128)(2,1)}, u32[]{:S(2)}) copy-start(bf16[768,512]{1,0:T(8,128)(2,1)} %copy-done.2) | copy-start | bytes 2359300
  162.6 30.5 %all-to-all-start.3 = ((bf16[8,1024,128]{1,2,0:T(8,128)(2,1)}), bf16[8,1024,128]{1,2,0:T(8,128)(2,1)}, u32[]{:S(2)}, u32[]{:S(2)}) async-start(bf16[8,1024,128]{1,2,0:T(8,128)(2,1)} %bitcast.80), calls=%async_computation.3 | async-start | bytes 4194304 | tf_op jit(solution)/shard_map/all_to_all | solution.py:193
  167.9 5.3 %collective-permute-start.6 = (bf16[768,512]{1,0:T(8,128)(2,1)S(1)}, bf16[768,512]{1,0:T(8,128)(2,1)}, u32[]{:S(2)}, u32[]{:S(2)}) collective-permute-start(bf16[768,512]{1,0:T(8,128)(2,1)S(1)} %copy-done.1), channel_id=1, source_target_pairs={{0,16},{16,0},{1,17},{17,1},{2,18},{18,2},{3,19},{19,3},{4,20},{20... | collective-permute-start | bytes 2359304 | tf_op jit(solution)/shard_map/ppermute | solution.py:44
  172.3 2.8 %copy-start.10 = (bf16[768,512]{1,0:T(8,128)(2,1)S(1)}, bf16[768,512]{1,0:T(8,128)(2,1)}, u32[]{:S(2)}) copy-start(bf16[768,512]{1,0:T(8,128)(2,1)} %copy-done.9) | copy-start | bytes 2359300
  175.1 1.2 copy-start.13
  193.1 30.8 %all-to-all-start.5 = ((bf16[8,1024,128]{1,2,0:T(8,128)(2,1)}), bf16[8,1024,128]{1,2,0:T(8,128)(2,1)}, u32[]{:S(2)}, u32[]{:S(2)}) async-start(bf16[8,1024,128]{1,2,0:T(8,128)(2,1)} %maximum_bitcast_fusion), calls=%async_computation.5 | async-start | bytes 4194304 | tf_op jit(solution)/shard_map/all_to_all | solution.py:193
  198.6 4.0 %copy-start.8 = (bf16[8,1024,128]{1,2,0:T(8,128)(2,1)S(1)}, bf16[8,1024,128]{1,2,0:T(8,128)(2,1)}, u32[]{:S(2)}) copy-start(bf16[8,1024,128]{1,2,0:T(8,128)(2,1)} %copy-done.6) | copy-start | bytes 6291460
  203.7 2.1 copy-start.4
  205.8 46.5 %collective-permute-start.10 = (f32[384,1024]{1,0:T(8,128)}, f32[384,1024]{1,0:T(8,128)}, u32[]{:S(2)}, u32[]{:S(2)}) collective-permute-start(f32[384,1024]{1,0:T(8,128)} %constant_dynamic-slice_fusion.3), channel_id=1, source_target_pairs={{0,16},{16,0},{1,17},{17,1},{2,18},{18,2},{3,19},{19,3},{4,20},{20... | collective-permute-start | bytes 4718600 | tf_op jit(solution)/shard_map/ppermute | solution.py:44
  212.3 18.6 %copy-start.17 = (bf16[768,512]{0,1:T(8,128)(2,1)S(1)}, bf16[768,512]{0,1:T(8,128)(2,1)}, u32[]{:S(2)}) copy-start(bf16[768,512]{0,1:T(8,128)(2,1)} %convolution_convert_fusion.4) | copy-start | bytes 2359300
  223.8 16.7 %all-to-all-start.4 = ((bf16[16,64,128]{2,1,0:T(8,128)(2,1)}), bf16[16,64,128]{2,1,0:T(8,128)(2,1)S(1)}, u32[]{:S(2)}, u32[]{:S(2)}) async-start(bf16[16,64,128]{2,1,0:T(8,128)(2,1)} %bitcast.27), calls=%async_computation.4 | async-start | bytes 524288 | tf_op jit(solution)/shard_map/all_to_all | solution.py:195
  231.0 15.1 %collective-permute-start.7 = (bf16[384,512]{0,1:T(8,128)(2,1)S(1)}, bf16[384,512]{0,1:T(8,128)(2,1)S(1)}, u32[]{:S(2)}, u32[]{:S(2)}) collective-permute-start(bf16[384,512]{0,1:T(8,128)(2,1)S(1)} %get-tuple-element.63), channel_id=1, source_target_pairs={{0,16},{16,0},{1,17},{17,1},{2,18},{18,2},{3,19},{19,3},{4,20},{20... | collective-permute-start | bytes 1179656 | tf_op jit(solution)/shard_map/ppermute | solution.py:44
  240.6 5.5 %copy-start.14 = (bf16[16,64,128]{2,1,0:T(8,128)(2,1)}, bf16[16,64,128]{2,1,0:T(8,128)(2,1)S(1)}, u32[]{:S(2)}) copy-start(bf16[16,64,128]{2,1,0:T(8,128)(2,1)S(1)} %all-to-all-done.4) | copy-start | bytes 786436
  240.6 15.4 %all-to-all-start.6 = ((bf16[16,64,128]{2,1,0:T(8,128)(2,1)}), bf16[16,64,128]{2,1,0:T(8,128)(2,1)}, u32[]{:S(2)}, u32[]{:S(2)}) async-start(bf16[16,64,128]{2,1,0:T(8,128)(2,1)} %bitcast.32), calls=%async_computation.6 | async-start | bytes 524288 | tf_op jit(solution)/shard_map/all_to_all | solution.py:195
  246.1 0.7 copy-start.20
  246.9 5.5 %copy-start.5 = (f32[768,1024]{1,0:T(8,128)S(1)}, f32[768,1024]{1,0:T(8,128)}, u32[]{:S(2)}) copy-start(f32[768,1024]{1,0:T(8,128)} %copy-done.4) | copy-start | bytes 9437188
  252.3 2.2 copy-start.15
  257.9 20.7 %all-to-all-start.7 = ((bf16[16,2,64,128]{3,2,1,0:T(8,128)(2,1)}), bf16[16,2,64,128]{3,2,1,0:T(8,128)(2,1)}, u32[]{:S(2)}, u32[]{:S(2)}) async-start(bf16[16,2,64,128]{3,2,1,0:T(8,128)(2,1)} %broadcast_in_dim.23), calls=%async_computation.7 | async-start | bytes 1048576 | tf_op jit(solution)/shard_map/all_to_all | solution.py:182
